TPU v7x, 32 devices: a whole 2x2x4 slice. The times are simulated.
32 devices in a mesh: groups: 2 (over y), users: 4 (over z), hours: 4 (over x, core).
Axes of the slice: x: 2, y: 2, z: 4, core: 2. Of those that a mesh axis runs over, the one named last changes fastest.
Arguments:
- activity: bfloat16 [16384, 8192], P(('groups', 'users'), 'hours'), parts along dimension 0, may hold values from -6 to 6
- cohort: int32 [16384], P(('groups', 'users')), parts along dimension 0, may hold values from 0 to 15
- tap_table: float32 [16, 9], replicated, may hold values from 0.02 to 0.4
- sketch: bfloat16 [8192, 64], P('hours'), may hold values from -0.0625 to 0.0625
Outputs:
- basis: float32 [16384, 64], P(('groups', 'users', 'hours')), parts along dimension 0
- triangle: float32 [128, 64], P('groups'), parts along dimension 0
There are 2 independent parts, one for each index of `groups`. A program takes and returns all parts, laid end to end along the dimension named above; an argument that names none is the same for every part. Nothing has to cross between parts.
All inputs are finite; a program needn't handle non-finite values.
Results may differ from a plain program's by a relative error of at most 0.003.
Values may be sent and summed in bfloat16 or wider, within the bound.
A program may use at most 64 MiB of HBM per device.

v0:
```python
import math
import jax
import jax.numpy as jnp
from jax import lax
from jax.sharding import PartitionSpec as P

TAPS = 9


def with_halo(block, sides, width):
    for axis, dim in sides:
        count = lax.axis_size(axis)
        forward = [(i, i + 1) for i in range(count - 1)]
        backward = [(target, source) for source, target in forward]
        low = lax.ppermute(
            lax.slice_in_dim(block, block.shape[dim] - width, None, axis=dim), axis, forward
        )
        high = lax.ppermute(lax.slice_in_dim(block, 0, width, axis=dim), axis, backward)
        block = jnp.concatenate([low, block, high], axis=dim)
    return block


def partner_2(value, axis, distance):
    mask = 2**distance
    pairs = [(source, source ^ mask) for source in range(lax.axis_size(axis))]
    return lax.ppermute(value, axis, pairs)


def per_device(activity, cohort, tap_table, sketch):
    rows = activity.shape[0]
    width = activity.shape[1]
    reach = (TAPS - 1) // 2
    padded = with_halo(activity, (("hours", 1),), reach)
    onehot = (cohort[:, None] == jnp.arange(tap_table.shape[0], dtype=jnp.int32)[None, :]).astype(
        jnp.float32
    )
    taps = jnp.dot(onehot, tap_table, precision=lax.Precision.HIGHEST)
    share = rows // lax.axis_size("hours")
    total = jnp.zeros((rows, width), jnp.float32)
    for step in range(TAPS):
        total = total + taps[:, step : step + 1] * padded[:, step : step + width].astype(
            jnp.float32
        )
    smoothed = total.astype(jnp.bfloat16)
    summed = lax.psum(jnp.dot(smoothed, sketch, preferred_element_type=jnp.float32), "hours")
    local = lax.dynamic_slice_in_dim(summed, lax.axis_index("hours") * share, share, 0)
    gram = jnp.dot(local.T, local, precision=lax.Precision.HIGHEST)
    lower = jnp.linalg.cholesky(gram)
    levels = lax.axis_size(("users", "hours")).bit_length() - 1
    for level in range(levels):
        partner = partner_2(lower, ("users", "hours"), level)
        joined = jnp.dot(lower, lower.T, precision=lax.Precision.HIGHEST) + jnp.dot(
            partner, partner.T, precision=lax.Precision.HIGHEST
        )
        lower = jnp.linalg.cholesky(joined)
    basis = lax.linalg.triangular_solve(lower, local, left_side=False, lower=True, transpose_a=True)
    scale = 1.0 / math.sqrt(rows * lax.axis_size("users"))
    triangle = lower.T * jnp.float32(scale)
    return (basis, triangle)


def solution(mesh):
    return jax.shard_map(
        per_device,
        mesh=mesh,
        in_specs=(P(("groups", "users"), "hours"), P(("groups", "users")), P(), P("hours", None)),
        out_specs=(P(("groups", "users", "hours"), None), P("groups", None)),
        check_vma=False,
    )
```

profile of v0, /device:TPU:0, one launch (start us, length us, event | category | flops | bytes accessed | tf_op | source)
XLA Modules:
  0.0 174.9 jit_solution(3421940850101160094)
XLA Ops:
  7.2 1.5 fusion.27
  8.7 2.4 %collective-permute-start = (bf16[2048,4]{1,0:T(8,128)(2,1)S(1)}, bf16[2048,4]{1,0:T(8,128)(2,1)S(1)}, u32[]{:S(2)}, u32[]{:S(2)}) collective-permute-start(bf16[2048,4]{1,0:T(8,128)(2,1)S(1)} %get-tuple-element.6), channel_id=1, source_target_pairs={{0,1},{1,2},{2,3},{4,5},{5,6},{6,7},{8,9},{9,10},{10,11},{12,13},{... | collective-permute-start | bytes 49160 | tf_op jit(solution)/shard_map/ppermute | solution.py:15
  11.1 1.3 collective-permute-start.1
  12.4 8.3 %constant_dynamic-update-slice_fusion.1 = bf16[2048,2052]{1,0:T(8,128)(2,1)} fusion(bf16[2048,2048]{1,0:T(8,128)(2,1)} %param.5), kind=kLoop, calls=%fused_computation.51 | loop fusion | bytes 16777216
  20.7 0.9 fusion.4
  21.8 0.9 constant_dynamic-update-slice_fusion
  22.7 47.5 %fusion.3 = f32[2048,64]{0,1:T(8,128)} fusion(bf16[2048,64]{0,1:T(8,128)(2,1)S(1)} %copy-done, bf16[2048,2048]{1,0:T(8,128)(2,1)} %param.5, bf16[2048,4]{1,0:T(8,128)(2,1)S(1)} %collective-permute-done, bf16[2048,2052]{1,0:T(8,128)(2,1)} %constant_dynamic-update-slice_fusion, f32[2048]{0:T(1024)S(1)} %bitcast.55, f32[2048]{0:T(1024)S(1)} %bitcast.56, ...), kind=kOutput, calls=%fused_computation.9 | convolution fusion | flops 700448768 | bytes 42819584 | tf_op jit(solution)/shard_map/dot_general | solution.py:45
  70.2 37.9 %all-reduce.2.cloned.1.call-done = f32[2048,64]{0,1:T(8,128)} async-done(((f32[2048,64]{0,1:T(8,128)}), f32[2048,64]{0,1:T(8,128)}) %all-reduce.2.cloned.1.call-update) | async-done | bytes 524304 | tf_op jit(solution)/shard_map/psum | solution.py:45
  108.1 1.2 fusion.8
  109.3 0.1 copy.6
  109.4 5.8 %cholesky.89 = f32[64,64]{1,0:T(8,128)S(1)} custom-call(f32[64,64]{1,0:T(8,128)S(1)} %fusion.15), custom_call_target="Cholesky" | custom-call | tf_op jit(solution)/shard_map/jit(cholesky)/cholesky | solution.py:48
  115.3 0.6 compare_reduce_fusion.4
  115.9 0.7 select_select_fusion.4
  116.6 0.1 collective-permute-start.2
  116.7 0.2 fusion.29
  116.9 1.0 collective-permute-done.2
  117.9 0.2 convolution_add_fusion.3
  118.1 0.1 copy.9
  118.2 5.8 %cholesky.100 = f32[64,64]{1,0:T(8,128)S(1)} custom-call(f32[64,64]{1,0:T(8,128)S(1)} %fusion.14), custom_call_target="Cholesky" | custom-call | tf_op jit(solution)/shard_map/jit(cholesky)/cholesky | solution.py:55
  124.0 0.6 compare_reduce_fusion.3
  124.7 0.7 select_select_fusion.3
  125.4 0.2 collective-permute-start.3
  125.5 0.2 fusion.30
  125.7 3.6 %collective-permute-done.3 = f32[64,64]{1,0:T(8,128)S(1)} collective-permute-done((f32[64,64]{1,0:T(8,128)S(1)}, f32[64,64]{1,0:T(8,128)S(1)}, u32[]{:S(2)}, u32[]{:S(2)}) %collective-permute-start.3) | collective-permute-done | bytes 16416 | tf_op jit(solution)/shard_map/ppermute | solution.py:26
  129.3 0.2 convolution_add_fusion.2
  129.5 0.1 copy.12
  129.6 5.8 %cholesky.111 = f32[64,64]{1,0:T(8,128)S(1)} custom-call(f32[64,64]{1,0:T(8,128)S(1)} %fusion.13), custom_call_target="Cholesky" | custom-call | tf_op jit(solution)/shard_map/jit(cholesky)/cholesky | solution.py:55
  135.5 0.6 compare_reduce_fusion.2
  136.1 0.7 select_select_fusion.2
  136.8 1.5 collective-permute-start.4
  138.4 0.2 fusion.31
  138.5 2.2 %collective-permute-done.4 = f32[64,64]{1,0:T(8,128)S(1)} collective-permute-done((f32[64,64]{1,0:T(8,128)S(1)}, f32[64,64]{1,0:T(8,128)S(1)}, u32[]{:S(2)}, u32[]{:S(2)}) %collective-permute-start.4) | collective-permute-done | bytes 16416 | tf_op jit(solution)/shard_map/ppermute | solution.py:26
  140.8 0.2 convolution_add_fusion.1
  141.0 0.1 copy.15
  141.1 5.8 %cholesky.122 = f32[64,64]{1,0:T(8,128)S(1)} custom-call(f32[64,64]{1,0:T(8,128)S(1)} %fusion.12), custom_call_target="Cholesky" | custom-call | tf_op jit(solution)/shard_map/jit(cholesky)/cholesky | solution.py:55
  147.0 0.6 compare_reduce_fusion.1
  147.6 0.7 select_select_fusion.1
  148.3 2.5 %collective-permute-start.5 = (f32[64,64]{1,0:T(8,128)S(1)}, f32[64,64]{1,0:T(8,128)S(1)}, u32[]{:S(2)}, u32[]{:S(2)}) collective-permute-start(f32[64,64]{1,0:T(8,128)S(1)} %select_select_fusion.1), channel_id=1, source_target_pairs={{0,8},{1,9},{2,10},{3,11},{4,12},{5,13},{6,14},{7,15},{8,0},{9,1},... | collective-permute-start | bytes 49160 | tf_op jit(solution)/shard_map/ppermute | solution.py:26
  150.7 0.2 fusion.32
  150.9 2.2 %collective-permute-done.5 = f32[64,64]{1,0:T(8,128)S(1)} collective-permute-done((f32[64,64]{1,0:T(8,128)S(1)}, f32[64,64]{1,0:T(8,128)S(1)}, u32[]{:S(2)}, u32[]{:S(2)}) %collective-permute-start.5) | collective-permute-done | bytes 16416 | tf_op jit(solution)/shard_map/ppermute | solution.py:26
  153.1 0.2 convolution_add_fusion
  153.3 0.1 copy.18
  153.4 5.8 %cholesky.133 = f32[64,64]{1,0:T(8,128)S(1)} custom-call(f32[64,64]{1,0:T(8,128)S(1)} %fusion.11), custom_call_target="Cholesky" | custom-call | tf_op jit(solution)/shard_map/jit(cholesky)/cholesky | solution.py:55
  159.3 0.6 compare_reduce_fusion
  160.0 0.7 multiply_bitcast_fusion
  160.6 4.9 %custom-call.5 = f32[1,64,64]{1,2,0:T(8,128)S(1)} custom-call(f32[1,64,64]{2,1,0:T(8,128)S(1)} %get-tuple-element.17), custom_call_target="InvertDiagBlocksLowerTriangular" | custom-call | tf_op jit(solution)/shard_map/triangular_solve | solution.py:56
  165.5 0.7 copy.19
  166.2 1.9 %fusion.6 = f32[512,64]{0,1:T(8,128)} fusion(f32[2048,64]{0,1:T(8,128)} %all-reduce.2.cloned.1.call-done, s32[]{:T(128)S(6)} %select_n.6, f32[1,64,64]{1,2,0:T(8,128)S(1)} %custom-call.5), kind=kOutput, calls=%fused_computation.17 | convolution fusion | flops 25165824 | bytes 278532 | tf_op jit(solution)/shard_map/triangular_solve | solution.py:56
  (21 shorter events, 0.3 us)
Async XLA Ops:
  7.2 15.5 %copy-start = (bf16[2048,64]{0,1:T(8,128)(2,1)S(1)}, bf16[2048,64]{0,1:T(8,128)(2,1)}, u32[]{:S(2)}) copy-start(bf16[2048,64]{0,1:T(8,128)(2,1)} %param.8) | copy-start | bytes 786436
  7.2 100.9 %all-reduce.2.cloned.1.call-start = ((), (), s32[]{:S(2)}) async-start(), calls=%async_computation | async-start | bytes 1048576 | tf_op jit(solution)/shard_map/psum | solution.py:45
  8.7 12.1 %copy-start.1 = (f32[16,9]{1,0:T(8,128)S(1)}, f32[16,9]{1,0:T(8,128)}, u32[]{:S(2)}) copy-start(f32[16,9]{1,0:T(8,128)} %param.7) | copy-start | bytes 1732
  8.7 12.1 %copy-start.2 = (s32[2048]{0:T(1024)S(1)}, s32[2048]{0:T(1024)}, u32[]{:S(2)}) copy-start(s32[2048]{0:T(1024)} %param.6) | copy-start | bytes 24580
  8.7 14.0 %collective-permute-start = (bf16[2048,4]{1,0:T(8,128)(2,1)S(1)}, bf16[2048,4]{1,0:T(8,128)(2,1)S(1)}, u32[]{:S(2)}, u32[]{:S(2)}) collective-permute-start(bf16[2048,4]{1,0:T(8,128)(2,1)S(1)} %get-tuple-element.6), channel_id=1, source_target_pairs={{0,1},{1,2},{2,3},{4,5},{5,6},{6,7},{8,9},{9,10},{10,11},{12,13},{... | collective-permute-start | bytes 49160 | tf_op jit(solution)/shard_map/ppermute | solution.py:15
  11.1 10.7 %collective-permute-start.1 = (bf16[2048,4]{1,0:T(8,128)(2,1)S(1)}, bf16[2048,4]{1,0:T(8,128)(2,1)S(1)}, u32[]{:S(2)}, u32[]{:S(2)}) collective-permute-start(bf16[2048,4]{1,0:T(8,128)(2,1)S(1)} %get-tuple-element.5), channel_id=1, source_target_pairs={{1,0},{2,1},{3,2},{5,4},{6,5},{7,6},{9,8},{10,9},{11,10},{13,12},{... | collective-permute-start | bytes 49160 | tf_op jit(solution)/shard_map/ppermute | solution.py:18
  116.6 1.3 collective-permute-start.2
  125.4 4.0 %collective-permute-start.3 = (f32[64,64]{1,0:T(8,128)S(1)}, f32[64,64]{1,0:T(8,128)S(1)}, u32[]{:S(2)}, u32[]{:S(2)}) collective-permute-start(f32[64,64]{1,0:T(8,128)S(1)} %select_select_fusion.3), channel_id=1, source_target_pairs={{0,2},{1,3},{2,0},{3,1},{4,6},{5,7},{6,4},{7,5},{8,10},{9,11},{10,... | collective-permute-start | bytes 49160 | tf_op jit(solution)/shard_map/ppermute | solution.py:26
  136.8 4.0 %collective-permute-start.4 = (f32[64,64]{1,0:T(8,128)S(1)}, f32[64,64]{1,0:T(8,128)S(1)}, u32[]{:S(2)}, u32[]{:S(2)}) collective-permute-start(f32[64,64]{1,0:T(8,128)S(1)} %select_select_fusion.2), channel_id=1, source_target_pairs={{0,4},{1,5},{2,6},{3,7},{4,0},{5,1},{6,2},{7,3},{8,12},{9,13},{10,... | collective-permute-start | bytes 49160 | tf_op jit(solution)/shard_map/ppermute | solution.py:26
  148.3 4.9 %collective-permute-start.5 = (f32[64,64]{1,0:T(8,128)S(1)}, f32[64,64]{1,0:T(8,128)S(1)}, u32[]{:S(2)}, u32[]{:S(2)}) collective-permute-start(f32[64,64]{1,0:T(8,128)S(1)} %select_select_fusion.1), channel_id=1, source_target_pairs={{0,8},{1,9},{2,10},{3,11},{4,12},{5,13},{6,14},{7,15},{8,0},{9,1},... | collective-permute-start | bytes 49160 | tf_op jit(solution)/shard_map/ppermute | solution.py:26
Sparse Core Ops, SparseCore 0:
  70.3 37.7 all-reduce.1
where the time goes:
time: 175 us
  matrix products  53 us (30%)
  waiting for transfers between devices  47 us (27%)
  other arithmetic  40.8 us (23%)
  between operations  14.3 us (8%)
  local copies, waits for them, and re-layouts  11.9 us (7%)
  starting transfers between devices  8 us (5%)
    dot_general x1, matrix products, per_device(): jnp.dot(smoothed, sketch, preferred_element_type=jnp.float32)  47.5 us
    psum x1, waiting for transfers between devices, per_device(): lax.psum(jnp.dot(smoothed, sketch, preferred_element_type=jnp.float32), '...  37.9 us
    another operation x12, other arithmetic, per_device(): lower = jnp.linalg.cholesky(joined)  26.1 us
    unnamed x8, local copies, waits for them, and re-layouts  9.07 us
    ppermute x4, waiting for transfers between devices, partner_2(): return lax.ppermute(value, axis, pairs)  9.06 us
    another operation x3, other arithmetic, per_device(): lower = jnp.linalg.cholesky(gram)  6.52 us
    another operation x1, other arithmetic, per_device(): lax.linalg.triangular_solve(lower, local, left_side=False, lower=True, tr...  4.9 us
    ppermute x4, starting transfers between devices, partner_2(): return lax.ppermute(value, axis, pairs)  4.28 us
  transfers between devices with their start and end apart: 7, of which 5 were waited for; matrix products, arithmetic and copies ran while one was open for 6% of the time, Pallas kernels for 0%

commit v1 on v0

--- a/solution.py
+++ b/solution.py
@@ -42,7 +42,10 @@
             jnp.float32
         )
     smoothed = total.astype(jnp.bfloat16)
-    summed = lax.psum(jnp.dot(smoothed, sketch, preferred_element_type=jnp.float32), "hours")
+    summed = jnp.sum(
+        lax.all_gather(jnp.dot(smoothed, sketch, preferred_element_type=jnp.float32), "hours"),
+        axis=0,
+    )
     local = lax.dynamic_slice_in_dim(summed, lax.axis_index("hours") * share, share, 0)
     gram = jnp.dot(local.T, local, precision=lax.Precision.HIGHEST)
     lower = jnp.linalg.cholesky(gram)

time: 175 us -> 167 us (0.954)
  waiting for transfers between devices: 47 us -> 36 us
  local copies, waits for them, and re-layouts: 11.9 us -> 14.7 us
  matrix products: 53 us -> 51.2 us
    psum x1 -> x0, waiting for transfers between devices: 37.9 us -> none  [per_device(): lax.psum(jnp.dot(smoothed, sketch, preferred_element_type=jnp.float32), '...]
    all_gather x0 -> x1, waiting for transfers between devices: none -> 27.3 us  [per_device(): lax.all_gather(jnp.dot(smoothed, sketch, preferred_element_type=jnp.float...]
    all_gather x0 -> x1, local copies, waits for them, and re-layouts: none -> 2.85 us  [per_device(): lax.all_gather(jnp.dot(smoothed, sketch, preferred_element_type=jnp.float...]
  transfers between devices with their start and end apart: 7 -> 7, of which waited for: 5 -> 5; matrix products, arithmetic and copies ran while one was open for 6% -> 7% of each run, Pallas kernels for 0% -> 0%
where the time goes in v1:
time: 167 us
  matrix products  51.2 us (31%)
  other arithmetic  42.1 us (25%)
  waiting for transfers between devices  36 us (22%)
  local copies, waits for them, and re-layouts  14.7 us (9%)
  between operations  14.3 us (9%)
  starting transfers between devices  8.42 us (5%)
    dot_general x1, matrix products, per_device(): jnp.dot(smoothed, sketch, preferred_element_type=jnp.float32)  47.5 us
    all_gather x1, waiting for transfers between devices, per_device(): lax.all_gather(jnp.dot(smoothed, sketch, preferred_element_type=jnp.float...  27.3 us
    another operation x12, other arithmetic, per_device(): lower = jnp.linalg.cholesky(joined)  26.1 us
    unnamed x8, local copies, waits for them, and re-layouts  9.05 us
    ppermute x4, waiting for transfers between devices, partner_2(): return lax.ppermute(value, axis, pairs)  8.64 us
    another operation x3, other arithmetic, per_device(): lower = jnp.linalg.cholesky(gram)  6.52 us
    another operation x1, other arithmetic, per_device(): lax.linalg.triangular_solve(lower, local, left_side=False, lower=True, tr...  4.9 us
    ppermute x4, starting transfers between devices, partner_2(): return lax.ppermute(value, axis, pairs)  4.7 us
  transfers between devices with their start and end apart: 7, of which 5 were waited for; matrix products, arithmetic and copies ran while one was open for 7% of the time, Pallas kernels for 0%

profile of v1, /device:TPU:0, one launch (start us, length us, event | category | flops | bytes accessed | tf_op | source)
XLA Modules:
  0.0 166.7 jit_solution(2018655122681251722)
XLA Ops:
  7.2 1.5 fusion.27
  8.7 2.4 %collective-permute-start = (bf16[2048,4]{1,0:T(8,128)(2,1)S(1)}, bf16[2048,4]{1,0:T(8,128)(2,1)S(1)}, u32[]{:S(2)}, u32[]{:S(2)}) collective-permute-start(bf16[2048,4]{1,0:T(8,128)(2,1)S(1)} %get-tuple-element.8), channel_id=1, source_target_pairs={{0,1},{1,2},{2,3},{4,5},{5,6},{6,7},{8,9},{9,10},{10,11},{12,13},{... | collective-permute-start | bytes 49160 | tf_op jit(solution)/shard_map/ppermute | solution.py:15
  11.1 1.3 collective-permute-start.1
  12.4 8.3 %constant_dynamic-update-slice_fusion.1 = bf16[2048,2052]{1,0:T(8,128)(2,1)} fusion(bf16[2048,2048]{1,0:T(8,128)(2,1)} %param.5), kind=kLoop, calls=%fused_computation.51 | loop fusion | bytes 16777216
  20.7 0.9 fusion.4
  21.8 0.9 constant_dynamic-update-slice_fusion
  22.7 47.5 %fusion.3 = f32[2048,64]{0,1:T(8,128)} fusion(bf16[2048,64]{0,1:T(8,128)(2,1)S(1)} %copy-done, bf16[2048,2048]{1,0:T(8,128)(2,1)} %param.5, bf16[2048,4]{1,0:T(8,128)(2,1)S(1)} %collective-permute-done, bf16[2048,2052]{1,0:T(8,128)(2,1)} %constant_dynamic-update-slice_fusion, f32[2048]{0:T(1024)S(1)} %bitcast.57, f32[2048]{0:T(1024)S(1)} %bitcast.58, ...), kind=kOutput, calls=%fused_computation.9 | convolution fusion | flops 700448768 | bytes 42819584 | tf_op jit(solution)/shard_map/dot_general | solution.py:46
  70.2 27.3 %all-gather.3.cloned.1.call-done = f32[8192,64]{0,1:T(8,128)} async-done(((f32[2048,64]{0,1:T(8,128)}), f32[8192,64]{0,1:T(8,128)}) %all-gather.3.cloned.1.call-update) | async-done | bytes 2097168 | tf_op jit(solution)/shard_map/all_gather | solution.py:46
  97.5 2.9 %reshape.13 = f32[4,2048,64]{1,0,2:T(4,128)S(1)} reshape(f32[8192,64]{0,1:T(8,128)} %all-gather.3.cloned.1.call-done) | data formatting | bytes 4194304 | tf_op jit(solution)/shard_map/all_gather | solution.py:46
  100.4 1.3 reduce_sum.9
  101.7 0.3 fusion.8
  102.0 0.1 copy.20
  102.1 5.8 %cholesky.89 = f32[64,64]{1,0:T(8,128)S(1)} custom-call(f32[64,64]{1,0:T(8,128)S(1)} %fusion.15), custom_call_target="Cholesky" | custom-call | tf_op jit(solution)/shard_map/jit(cholesky)/cholesky | solution.py:51
  108.0 0.6 compare_reduce_fusion.4
  108.6 0.7 select_select_fusion.4
  109.3 0.3 collective-permute-start.2
  109.6 0.2 fusion.29
  109.8 0.8 collective-permute-done.2
  110.5 0.2 convolution_add_fusion.3
  110.7 0.1 copy.23
  110.8 5.8 %cholesky.100 = f32[64,64]{1,0:T(8,128)S(1)} custom-call(f32[64,64]{1,0:T(8,128)S(1)} %fusion.14), custom_call_target="Cholesky" | custom-call | tf_op jit(solution)/shard_map/jit(cholesky)/cholesky | solution.py:58
  116.7 0.6 compare_reduce_fusion.3
  117.3 0.7 select_select_fusion.3
  118.0 0.4 collective-permute-start.3
  118.4 0.2 fusion.30
  118.6 3.4 %collective-permute-done.3 = f32[64,64]{1,0:T(8,128)S(1)} collective-permute-done((f32[64,64]{1,0:T(8,128)S(1)}, f32[64,64]{1,0:T(8,128)S(1)}, u32[]{:S(2)}, u32[]{:S(2)}) %collective-permute-start.3) | collective-permute-done | bytes 16416 | tf_op jit(solution)/shard_map/ppermute | solution.py:26
  122.0 0.2 convolution_add_fusion.2
  122.3 5.8 %cholesky.111 = f32[64,64]{1,0:T(8,128)S(1)} custom-call(f32[64,64]{1,0:T(8,128)S(1)} %fusion.13), custom_call_target="Cholesky" | custom-call | tf_op jit(solution)/shard_map/jit(cholesky)/cholesky | solution.py:58
  128.2 0.6 compare_reduce_fusion.2
  128.8 0.7 select_select_fusion.2
  129.5 1.5 collective-permute-start.4
  131.0 0.2 fusion.31
  131.2 2.2 %collective-permute-done.4 = f32[64,64]{1,0:T(8,128)S(1)} collective-permute-done((f32[64,64]{1,0:T(8,128)S(1)}, f32[64,64]{1,0:T(8,128)S(1)}, u32[]{:S(2)}, u32[]{:S(2)}) %collective-permute-start.4) | collective-permute-done | bytes 16416 | tf_op jit(solution)/shard_map/ppermute | solution.py:26
  133.4 0.2 convolution_add_fusion.1
  133.6 0.1 copy.29
  133.7 5.8 %cholesky.122 = f32[64,64]{1,0:T(8,128)S(1)} custom-call(f32[64,64]{1,0:T(8,128)S(1)} %fusion.12), custom_call_target="Cholesky" | custom-call | tf_op jit(solution)/shard_map/jit(cholesky)/cholesky | solution.py:58
  139.6 0.6 compare_reduce_fusion.1
  140.2 0.7 select_select_fusion.1
  140.9 2.5 %collective-permute-start.5 = (f32[64,64]{1,0:T(8,128)S(1)}, f32[64,64]{1,0:T(8,128)S(1)}, u32[]{:S(2)}, u32[]{:S(2)}) collective-permute-start(f32[64,64]{1,0:T(8,128)S(1)} %select_select_fusion.1), channel_id=1, source_target_pairs={{0,8},{1,9},{2,10},{3,11},{4,12},{5,13},{6,14},{7,15},{8,0},{9,1},... | collective-permute-start | bytes 49160 | tf_op jit(solution)/shard_map/ppermute | solution.py:26
  143.4 0.2 fusion.32
  143.6 2.2 %collective-permute-done.5 = f32[64,64]{1,0:T(8,128)S(1)} collective-permute-done((f32[64,64]{1,0:T(8,128)S(1)}, f32[64,64]{1,0:T(8,128)S(1)}, u32[]{:S(2)}, u32[]{:S(2)}) %collective-permute-start.5) | collective-permute-done | bytes 16416 | tf_op jit(solution)/shard_map/ppermute | solution.py:26
  145.8 0.2 convolution_add_fusion
  146.1 5.8 %cholesky.133 = f32[64,64]{1,0:T(8,128)S(1)} custom-call(f32[64,64]{1,0:T(8,128)S(1)} %fusion.11), custom_call_target="Cholesky" | custom-call | tf_op jit(solution)/shard_map/jit(cholesky)/cholesky | solution.py:58
  152.0 0.6 compare_reduce_fusion
  152.6 0.7 multiply_bitcast_fusion
  153.3 4.9 %custom-call.5 = f32[1,64,64]{1,2,0:T(8,128)S(1)} custom-call(f32[1,64,64]{2,1,0:T(8,128)S(1)} %get-tuple-element.19), custom_call_target="InvertDiagBlocksLowerTriangular" | custom-call | tf_op jit(solution)/shard_map/triangular_solve | solution.py:59
  158.2 1.0 fusion.6
  159.2 0.7 copy.33
  (23 shorter events, 0.5 us)
Async XLA Ops:
  7.2 15.5 %copy-start = (bf16[2048,64]{0,1:T(8,128)(2,1)S(1)}, bf16[2048,64]{0,1:T(8,128)(2,1)}, u32[]{:S(2)}) copy-start(bf16[2048,64]{0,1:T(8,128)(2,1)} %param.8) | copy-start | bytes 786436
  7.2 90.3 %all-gather.3.cloned.1.call-start = ((), (), s32[]{:S(2)}) async-start(), calls=%async_computation | async-start | bytes 2621440 | tf_op jit(solution)/shard_map/all_gather | solution.py:46
  8.7 12.1 %copy-start.1 = (f32[16,9]{1,0:T(8,128)S(1)}, f32[16,9]{1,0:T(8,128)}, u32[]{:S(2)}) copy-start(f32[16,9]{1,0:T(8,128)} %param.7) | copy-start | bytes 1732
  8.7 12.1 %copy-start.2 = (s32[2048]{0:T(1024)S(1)}, s32[2048]{0:T(1024)}, u32[]{:S(2)}) copy-start(s32[2048]{0:T(1024)} %param.6) | copy-start | bytes 24580
  8.7 14.0 %collective-permute-start = (bf16[2048,4]{1,0:T(8,128)(2,1)S(1)}, bf16[2048,4]{1,0:T(8,128)(2,1)S(1)}, u32[]{:S(2)}, u32[]{:S(2)}) collective-permute-start(bf16[2048,4]{1,0:T(8,128)(2,1)S(1)} %get-tuple-element.8), channel_id=1, source_target_pairs={{0,1},{1,2},{2,3},{4,5},{5,6},{6,7},{8,9},{9,10},{10,11},{12,13},{... | collective-permute-start | bytes 49160 | tf_op jit(solution)/shard_map/ppermute | solution.py:15
  11.1 10.7 %collective-permute-start.1 = (bf16[2048,4]{1,0:T(8,128)(2,1)S(1)}, bf16[2048,4]{1,0:T(8,128)(2,1)S(1)}, u32[]{:S(2)}, u32[]{:S(2)}) collective-permute-start(bf16[2048,4]{1,0:T(8,128)(2,1)S(1)} %get-tuple-element.7), channel_id=1, source_target_pairs={{1,0},{2,1},{3,2},{5,4},{6,5},{7,6},{9,8},{10,9},{11,10},{13,12},{... | collective-permute-start | bytes 49160 | tf_op jit(solution)/shard_map/ppermute | solution.py:18
  109.3 1.3 collective-permute-start.2
  118.0 4.0 %collective-permute-start.3 = (f32[64,64]{1,0:T(8,128)S(1)}, f32[64,64]{1,0:T(8,128)S(1)}, u32[]{:S(2)}, u32[]{:S(2)}) collective-permute-start(f32[64,64]{1,0:T(8,128)S(1)} %select_select_fusion.3), channel_id=1, source_target_pairs={{0,2},{1,3},{2,0},{3,1},{4,6},{5,7},{6,4},{7,5},{8,10},{9,11},{10,... | collective-permute-start | bytes 49160 | tf_op jit(solution)/shard_map/ppermute | solution.py:26
  129.5 4.0 %collective-permute-start.4 = (f32[64,64]{1,0:T(8,128)S(1)}, f32[64,64]{1,0:T(8,128)S(1)}, u32[]{:S(2)}, u32[]{:S(2)}) collective-permute-start(f32[64,64]{1,0:T(8,128)S(1)} %select_select_fusion.2), channel_id=1, source_target_pairs={{0,4},{1,5},{2,6},{3,7},{4,0},{5,1},{6,2},{7,3},{8,12},{9,13},{10,... | collective-permute-start | bytes 49160 | tf_op jit(solution)/shard_map/ppermute | solution.py:26
  140.9 4.9 %collective-permute-start.5 = (f32[64,64]{1,0:T(8,128)S(1)}, f32[64,64]{1,0:T(8,128)S(1)}, u32[]{:S(2)}, u32[]{:S(2)}) collective-permute-start(f32[64,64]{1,0:T(8,128)S(1)} %select_select_fusion.1), channel_id=1, source_target_pairs={{0,8},{1,9},{2,10},{3,11},{4,12},{5,13},{6,14},{7,15},{8,0},{9,1},... | collective-permute-start | bytes 49160 | tf_op jit(solution)/shard_map/ppermute | solution.py:26
Sparse Core Ops, SparseCore 0:
  70.3 27.1 all-gather.2
